TPU v7x, 32 devices: a whole 2x2x4 slice. The times are simulated.
32 devices in a mesh: group: 2 (over x), tok: 16 (over z, y, core).
Axes of the slice: x: 2, y: 2, z: 4, core: 2. Of those that a mesh axis runs over, the one named last changes fastest.
Arguments:
- initial_guess: float32 [512, 16, 128], P(('group', 'tok')), parts along dimension 0, may hold values from -6 to 6
- noise_draws: float32 [512, 16, 128], P(('group', 'tok')), parts along dimension 0, may hold values from -6 to 6
- drift_state: float32 [16], replicated, may hold values from 0 to 0.15
- drift_denoise: float32 [16], replicated, may hold values from -0.4 to -0.15
- noise_scale: float32 [16], replicated, may hold values from 0.05 to 0.3
- modulation: float32 [16, 8, 1152], replicated, may hold values from -3 to 3
- embed_weight: bfloat16 [16, 1152], replicated, may hold values from -1.5 to 1.5
- space_input: bfloat16 [1152, 1728], replicated, may hold values from -0.1875 to 0.1875
- space_output: bfloat16 [576, 1152], replicated, may hold values from -0.25 to 0.25
- time_input: bfloat16 [1152, 1728], replicated, may hold values from -0.1875 to 0.1875
- time_output: bfloat16 [576, 1152], replicated, may hold values from -0.25 to 0.25
- final_weight: bfloat16 [1152, 16], replicated, may hold values from -0.1875 to 0.1875
Outputs:
- next_states: float32 [512, 16, 128], P(('group', 'tok')), parts along dimension 0
There are 2 independent parts, one for each index of `group`. A program takes and returns all parts, laid end to end along the dimension named above; an argument that names none is the same for every part. Nothing has to cross between parts.
All inputs are finite; a program needn't handle non-finite values.
Results may differ from a plain program's by a relative error of at most 0.006.
Values may be sent and summed in bfloat16 or wider, within the bound.
No kernel may reach another device: no remote copies, remote signals or barrier semaphores. Data moves between devices by JAX's collectives and lax.ppermute only.
A program may use at most 128 MiB of HBM per device.

v0:
```python
import functools
import itertools
import math

import jax
import jax.numpy as jnp
from jax import lax
from jax.experimental import pallas as pl
from jax.experimental.pallas import tpu as pltpu
from jax.sharding import PartitionSpec as P

HEADS = 8
ITERS = 2
LANES = 128
ROWS8 = 8
ROWS16 = 16
F32 = jnp.float32
BF16 = jnp.bfloat16


def layer_norm(values):
    center = values - jnp.mean(values, -1, keepdims=True)
    return center * lax.rsqrt(jnp.mean(center * center, -1, keepdims=True) + 1e-06)


def normed_head(values, head_size, scale):
    total = jnp.sum(values * values, 0, keepdims=True)
    return values * (lax.rsqrt(total * (1.0 / head_size) + 1e-06) * scale)


def padded(values, fill, rows):
    extra = rows - values.shape[0]
    return jnp.concatenate(
        [values, jnp.full((extra, values.shape[1]), fill, F32)], 0
    ).astype(BF16)


def on_diagonal(blocks):
    zero = jnp.zeros_like(blocks[0])
    return jnp.concatenate(
        [
            jnp.concatenate([block if at == own else zero for at in range(len(blocks))], 1)
            for own, block in enumerate(blocks)
        ],
        0,
    )


def modulated_norm(values, rows_of, shift, scale):
    return (
        layer_norm(values) * (1.0 + rows_of[scale : scale + 1]) + rows_of[shift : shift + 1]
    ).astype(BF16)


def weave(main, side, main_count, side_count):
    done = 0
    for index, _ in enumerate(main):
        due = -(-(index + 1) * side_count // main_count)
        while done < due:
            next(side, None)
            done += 1
    for _ in side:
        pass


def attention_pieces(normed, input_turned, output_weight, same_position, places, groups, finish):
    query_rows, turned_keys, value_rows, kept, attended, turned_attended = places
    inner, width = output_weight.shape
    tokens = normed.shape[0]
    head_size = inner // HEADS
    deep, tall = query_rows.shape[1], value_rows.shape[1]
    chunk = HEADS // 2
    scale = head_size ** (-0.5) * math.log2(math.e)

    def project(kind):
        rows = input_turned[kind * inner : (kind + 1) * inner]
        return lax.dot_general(
            rows, normed[...], (((1,), (1,)), ((), ())), preferred_element_type=F32
        )

    def keep_projected(kind, packed):
        for head in range(HEADS):
            values = packed[head * head_size : (head + 1) * head_size]
            if kind == 0:
                query_rows[head] = padded(normed_head(values, head_size, scale), 0.0, deep)
            elif kind == 1:
                turned_keys[head] = padded(normed_head(values, head_size, 1.0), 0.0, deep).T
            else:
                value_rows[head] = padded(values, 1.0, tall)

    pairs = [groups[at : at + 2] for at in range(0, len(groups), 2)]

    def over(pair):
        return slice(pair[0].start, pair[-1].stop)

    def score(head, pair):
        return jnp.dot(
            jnp.concatenate([turned_keys[head, group] for group in pair], 1),
            on_diagonal([query_rows[head, :, group] for group in pair]),
            preferred_element_type=F32,
        )

    def keep_scored(head, pair, scores):
        weights = jnp.exp2(scores).astype(BF16)
        if same_position is not None:
            weights = weights * same_position[:, : weights.shape[1]]
        kept[head, :, over(pair)] = weights

    def mix(head, pair):
        return jnp.dot(
            value_rows[head, :, over(pair)],
            on_diagonal([kept[head, :, group] for group in pair]),
            preferred_element_type=F32,
        )

    def keep_mixed(head, pair, mixed):
        rate = 1.0 / mixed[head_size : head_size + ROWS8]
        parts = mixed[:head_size].reshape(head_size // ROWS8, ROWS8, -1) * rate[None]
        first, last = head * head_size, (head + 1) * head_size
        columns = over(pair)
        attended[first:last, columns] = parts.reshape(head_size, -1)
        for at in range(0, inner, LANES):
            stop = min(at + LANES, inner)
            if first < stop <= last:
                turned_attended[columns, at:stop] = attended[at:stop, columns].astype(BF16).T

    def projections(kind):
        return (lambda: project(kind)), (lambda got: keep_projected(kind, got))

    def scorings(head, pair):
        return (lambda: score(head, pair)), (lambda got: keep_scored(head, pair, got))

    def mixings(head, pair):
        return (lambda: mix(head, pair)), (lambda got: keep_mixed(head, pair, got))

    def outputs(at):
        columns = slice(at, min(at + 2 * LANES, width))
        return (
            lambda: jnp.dot(
                turned_attended[...], output_weight[:, columns], preferred_element_type=F32
            )
        ), (lambda got: finish(columns, got))

    every = [(head, pair) for head in range(HEADS) for pair in pairs]
    scored = [scorings(*at) for at in every]
    mixes = [mixings(*at) for at in every]
    first = [projections(0), projections(1), projections(2), scored[0]]
    behind = scored[1:]
    for index, task in enumerate(behind):
        first.append(task)
        if index >= 1:
            first.append(mixes[index - 1])
    first += mixes[len(behind) - 1 :]
    for tasks in (first, [outputs(at) for at in range(0, width, 2 * LANES)]):
        waiting = None
        for issue, use in tasks:
            got = issue()
            if waiting is not None:
                waiting[0](waiting[1])
            waiting = (use, got)
            yield
        waiting[0](waiting[1])
        yield


def main_pieces(groups, width):
    return 3 + HEADS * -(-groups // 2) * 2 + 1 + -(-width // (2 * LANES)) + 1


def run_pipelined(steps, before, main, behind, main_count, before_count, behind_count, ready):
    def one(index, own, last):
        following = jnp.minimum(index + 1, last)
        previous = jnp.maximum(index - 1, 0)
        side = itertools.chain(behind(previous, 1 - own), before(following, 1 - own))
        weave(main(index, own), side, main_count, before_count + behind_count)

    for _ in before(0, 0):
        pass
    ready()
    if steps % 2 == 0:

        @pl.loop(0, steps // 2)
        def _(turn_index):
            one(2 * turn_index, 0, steps - 1)
            one(2 * turn_index + 1, 1, steps - 1)

        for _ in behind(steps - 1, 1):
            pass
    else:
        for index in range(steps):
            one(index, index % 2, steps - 1)
        for _ in behind(steps - 1, (steps - 1) % 2):
            pass


BLOCK = 32


def run_space(latent, embed, rows_of, input_weight, output_weight, out, places, ready):
    frames, _, spatial = latent.shape
    width = embed.shape[1]
    step = groups_of(frames)
    tokens = step * spatial
    normed, base, inner_places = places[:2], places[2:4], places[4:]
    groups = [slice(at, at + spatial) for at in range(0, tokens, spatial)]

    def before(index, own):
        for frame in range(step):
            base[own][groups[frame]] = lax.dot_general(
                latent[index * step + frame].astype(BF16),
                embed[...],
                (((0,), (0,)), ((), ())),
                preferred_element_type=F32,
            )
            yield
        for at in range(0, tokens, BLOCK):
            normed[own][at : at + BLOCK] = modulated_norm(
                base[own][at : at + BLOCK], rows_of, 0, 1
            )
            yield

    def main(index, own):
        def finish(columns, mixed):
            after = base[own][:, columns] + rows_of[2:3, columns] * mixed
            for frame, group in enumerate(groups):
                out[index * step + frame, :, columns] = after[group].astype(out.dtype)

        return attention_pieces(
            normed[own], input_weight, output_weight, None, inner_places, groups, finish
        )

    def behind(index, own):
        return iter(())

    run_pipelined(
        frames // step, before, main, behind, main_pieces(step, width), step + tokens // BLOCK, 0, ready
    )


def run_time(after, rows_of, input_weight, output_weight, final, out, places, ready):
    frames, positions, width = after.shape
    step = groups_of(positions // ROWS8)
    rows = frames * ROWS8
    tokens = step * rows
    normed, settled, inner_places = places[:2], places[2:4], places[4:]
    groups = [slice(at, at + rows) for at in range(0, tokens, rows)]
    same_position = same_position_mask(frames, min(step, 2))

    def eight(index, group):
        at = (index * step + group) * ROWS8
        if not isinstance(at, int):
            at = pl.multiple_of(at, ROWS8)
        return pl.ds(at, ROWS8)

    def before(index, own):
        for group in range(step):
            for at in range(0, rows, BLOCK):
                some = slice(at // ROWS8, (at + BLOCK) // ROWS8)
                hidden = after[some, eight(index, group), :].reshape(BLOCK, width)
                first = groups[group].start + at
                normed[own][first : first + BLOCK] = modulated_norm(hidden, rows_of, 3, 4)
                yield

    def main(index, own):
        def finish(columns, mixed):
            for group in range(step):
                hidden = after[:, eight(index, group), columns].reshape(rows, -1)
                settled[own][groups[group], columns] = (
                    hidden + rows_of[5:6, columns] * mixed[groups[group]]
                )

        return attention_pieces(
            normed[own], input_weight, output_weight, same_position, inner_places, groups, finish
        )

    def behind(index, own):
        for group in range(step):
            for at in range(0, rows, BLOCK):
                first = groups[group].start + at
                last = modulated_norm(settled[own][first : first + BLOCK], rows_of, 6, 7)
                predicted = lax.dot_general(
                    last, final[...], (((1,), (1,)), ((), ())), preferred_element_type=F32
                )
                some = slice(at // ROWS8, (at + BLOCK) // ROWS8)
                out[some, eight(index, group), :] = predicted.reshape(
                    BLOCK // ROWS8, ROWS8, predicted.shape[1]
                )
                yield

    settled[1][...] = jnp.zeros_like(settled[1])
    run_pipelined(
        positions // (step * ROWS8), before, main, behind, main_pieces(step, width),
        tokens // BLOCK, tokens // BLOCK, ready,
    )


def same_position_mask(frames, count):
    shape = (frames * ROWS8, count * frames * ROWS8)
    row = lax.broadcasted_iota(jnp.int32, shape, 0) % ROWS8
    column = lax.broadcasted_iota(jnp.int32, shape, 1) % ROWS8
    return jnp.where(row == column, 1.0, 0.0).astype(BF16)


def groups_of(blocks):
    return next(step for step in (4, 2, 1) if blocks % step == 0)


def fused_kernel(
    timestep, rate_state, rate_denoise, rate_noise, latent, noise, modulation, embed,
    space_in_hbm, space_out_hbm, time_in_hbm, time_out_hbm, final, increment, rounded,
    rows_of, space_in, space_out, time_in, time_out, after, staged, sems, *turned,
):
    own = timestep[0]
    copies = [
        pltpu.make_async_copy(source, target, sems.at[index])
        for index, (source, target) in enumerate(
            (
                (modulation.at[own], rows_of),
                (space_in_hbm, space_in),
                (space_out_hbm, space_out),
                (time_in_hbm, time_in),
                (time_out_hbm, time_out),
            )
        )
    ]
    for copy in copies:
        copy.start()

    def wait_for(some):
        for copy in some:
            copy.wait()

    wait_for(copies[:1])
    run_space(
        latent, embed, rows_of, space_in, space_out, after, turned, lambda: wait_for(copies[1:3])
    )
    run_time(
        after, rows_of, time_in, time_out, final, staged, turned, lambda: wait_for(copies[3:])
    )
    keep = rate_state[own] + jnp.where(own == 0, 1.0, 0.0)
    for frame in range(latent.shape[0]):
        value = (
            keep * latent[frame]
            + rate_denoise[own] * staged[frame].T
            + rate_noise[own] * noise[frame]
        )
        increment[frame] = value
        rounded[frame] = value.astype(BF16)


def space_kernel(latent, rows_of, embed, space_in, space_out, after, *turned):
    run_space(latent, embed, rows_of, space_in, space_out, after, turned, lambda: None)


def time_kernel(after, rows_of, time_in, time_out, final, predicted, *turned):
    run_time(after, rows_of, time_in, time_out, final, predicted, turned, lambda: None)


def vmem(count):
    return [pl.BlockSpec(memory_space=pltpu.VMEM)] * count


PARAMS = dict(compiler_params=pltpu.CompilerParams(vmem_limit_bytes=56 * 2**20))


def turned_scratch(tokens, group_rows, width, inner):
    head_size = inner // HEADS
    deep = -(-head_size // LANES) * LANES
    tall = head_size + ROWS16 - head_size % ROWS16
    return [
        pltpu.VMEM((tokens, width), BF16),
        pltpu.VMEM((tokens, width), BF16),
        pltpu.VMEM((tokens, width), F32),
        pltpu.VMEM((tokens, width), F32),
        pltpu.VMEM((HEADS, deep, tokens), BF16),
        pltpu.VMEM((HEADS, tokens, deep), BF16),
        pltpu.VMEM((HEADS, tall, tokens), BF16),
        pltpu.VMEM((HEADS, group_rows, tokens), BF16),
        pltpu.VMEM((inner, tokens), F32),
        pltpu.VMEM((tokens, inner), BF16),
    ]


def scalars(count):
    return [pl.BlockSpec(memory_space=pltpu.SMEM)] * count


def step_fused(timestep, rates, latent, noise, modulation, weights):
    frames, channels, spatial = latent.shape
    embed, space_in, space_out, time_in, time_out, final = weights
    width = embed.shape[1]
    return pl.pallas_call(
        fused_kernel,
        out_shape=[
            jax.ShapeDtypeStruct(latent.shape, F32),
            jax.ShapeDtypeStruct(latent.shape, BF16),
        ],
        in_specs=scalars(4)
        + vmem(2)
        + [pl.BlockSpec(memory_space=pl.ANY)]
        + vmem(1)
        + [pl.BlockSpec(memory_space=pl.ANY)] * 4
        + vmem(1),
        out_specs=vmem(2),
        scratch_shapes=[
            pltpu.VMEM(modulation.shape[1:], F32),
            pltpu.VMEM(space_in.shape, BF16),
            pltpu.VMEM(space_out.shape, BF16),
            pltpu.VMEM(time_in.shape, BF16),
            pltpu.VMEM(time_out.shape, BF16),
            pltpu.VMEM((frames, spatial, width), F32),
            pltpu.VMEM((frames, spatial, channels), F32),
            pltpu.SemaphoreType.DMA((5,)),
        ]
        + turned_scratch(groups_of(frames) * spatial, spatial, width, space_out.shape[0]),
        name="denoise",
        **PARAMS,
    )(
        timestep, *rates, latent, noise, modulation, embed, space_in, space_out, time_in,
        time_out, final,
    )


def step_split(timestep, rates, latent, noise, modulation, weights, peers):
    frames, channels, spatial = latent.shape
    embed, space_in, space_out, time_in, time_out, final = weights
    width = embed.shape[1]
    own = timestep[0]
    rows_of = lax.dynamic_index_in_dim(modulation, own, 0, keepdims=False)
    after = pl.pallas_call(
        space_kernel,
        out_shape=jax.ShapeDtypeStruct((frames, spatial, width), BF16),
        in_specs=vmem(5),
        out_specs=vmem(1)[0],
        scratch_shapes=turned_scratch(groups_of(frames) * spatial, spatial, width, space_out.shape[0]),
        name="space",
        **PARAMS,
    )(latent, rows_of, embed, space_in, space_out)
    after = lax.all_to_all(
        after, "tok", split_axis=1, concat_axis=0, tiled=True, axis_index_groups=peers
    )
    predicted = pl.pallas_call(
        time_kernel,
        out_shape=jax.ShapeDtypeStruct(after.shape[:2] + (channels,), F32),
        in_specs=vmem(5),
        out_specs=vmem(1)[0],
        scratch_shapes=turned_scratch(
            groups_of(after.shape[1] // ROWS8) * ROWS8 * after.shape[0], ROWS8 * after.shape[0],
            width, time_out.shape[0],
        ),
        name="time",
        **PARAMS,
    )(after.astype(F32), rows_of, time_in, time_out, final)
    predicted = lax.all_to_all(
        predicted, "tok", split_axis=0, concat_axis=1, tiled=True, axis_index_groups=peers
    )
    rate_state, rate_denoise, rate_noise = (rate[own] for rate in rates)
    increment = (
        (rate_state + jnp.where(own == 0, 1.0, 0.0)) * latent
        + rate_denoise * jnp.swapaxes(predicted, 1, 2)
        + rate_noise * noise
    )
    return increment, increment.astype(BF16)


RADIX = 4


def sum_before(values, held, timesteps, groups):
    before = jnp.zeros_like(values)
    reach = 1
    while reach < timesteps:
        arrived = []
        for back in range(reach, min(reach * RADIX, timesteps), reach):
            moves = [
                (step * groups + block, (step + back) * groups + block)
                for step in range(timesteps - back)
                for block in range(groups)
            ]
            arrived.append(lax.ppermute(held, "tok", moves))
        for part in arrived:
            before = before + part.astype(F32)
        held = (values + before).astype(BF16)
        reach *= RADIX
    return before


def body(
    initial_guess,
    noise_draws,
    drift_state,
    drift_denoise,
    noise_scale,
    modulation,
    embed_weight,
    space_input,
    space_output,
    time_input,
    time_output,
    final_weight,
):
    timesteps = modulation.shape[0]
    devices = lax.axis_size("tok")
    groups = devices // timesteps
    timestep = lax.axis_index("tok") // groups
    leading = timestep == 0
    own = timestep.astype(jnp.int32).reshape(1)
    if groups == 1:
        step = step_fused
    else:
        peers = [[row * groups + block for block in range(groups)] for row in range(timesteps)]
        step = functools.partial(step_split, peers=peers)
    rates = (drift_state, drift_denoise, noise_scale)
    weights = (
        embed_weight, space_input.T, space_output, time_input.T, time_output, final_weight.T
    )

    def iterate(_, held):
        latent = held[0]
        increment, rounded = step(own, rates, latent, noise_draws, modulation, weights)
        before = sum_before(increment, rounded, timesteps, groups)
        return jnp.where(leading, latent, before), before + increment

    return lax.fori_loop(0, ITERS, iterate, (initial_guess, initial_guess))[1]


def solution(mesh):
    rows = P(("group", "tok"), None, None)
    placed = (rows, rows) + (P(),) * 10
    return jax.shard_map(
        body, mesh=mesh, in_specs=placed, out_specs=rows, check_vma=False
    )
```

profile of v0, /device:TPU:0, one launch (start us, length us, event | category | flops | bytes accessed | tf_op | source)
XLA Modules:
  0.0 152.1 jit_solution(13114625470043417054)
XLA Ops:
  0.0 0.9 copy.24
  0.9 0.7 copy.15
  1.6 150.6 %while.12 = (s32[]{:T(128)}, f32[16,16,128]{2,1,0:T(8,128)S(1)}, f32[16,16,128]{2,1,0:T(8,128)}, pred[]{:T(512)}, s32[1]{0:T(128)}, /*index=5*/f32[16]{0:T(128)}...) while((s32[]{:T(128)}, f32[16,16,128]{2,1,0:T(8,128)S(1)}, ...), condition=%wide.region_1.2_spmd, body=%wide.region_0.1_spmd.sunk | while | flops 655362 | bytes 2883982 | solution.py:524
  1.6 48.8 %denoise.1 = (f32[16,16,128]{2,1,0:T(8,128)}, bf16[16,16,128]{2,1,0:T(8,128)(2,1)}) custom-call(s32[1]{0:T(128)} %get-tuple-element.264.timestep, f32[16]{0:T(128)} %get-tuple-element.265.rate_state, f32[16]{0:T(128)} %get-tuple-element.266.rate_denoise, f32[16]{0:T(128)} %get-tuple-element.267.rate_noise, f32[16,16,128]{2,1,0:T(8,128)S(1)} %get-tuple-element.244.latent, ...), custom_call_target="tpu_custom_call" | custom-call | tf_op jit(solution)/shard_map/while/body/eval_jaxpr/denoise/pallas_call | solution.py:392
  50.4 2.4 %collective-permute-start.2 = (bf16[16,16,128]{2,1,0:T(8,128)(2,1)}, bf16[16,16,128]{2,1,0:T(8,128)(2,1)S(1)}, u32[]{:S(2)}, u32[]{:S(2)}) collective-permute-start(bf16[16,16,128]{2,1,0:T(8,128)(2,1)} %get-tuple-element.223), channel_id=1, source_target_pairs={{0,1},{1,2},{2,3},{3,4},{4,5},{5,6},{6,7},{7,8},{8,9},{9,10},{10,1... | collective-permute-start | bytes 196616 | tf_op jit(solution)/shard_map/while/body/eval_jaxpr/ppermute | solution.py:480
  52.8 4.4 %collective-permute-start.1 = (bf16[16,16,128]{2,1,0:T(8,128)(2,1)}, bf16[16,16,128]{2,1,0:T(8,128)(2,1)S(1)}, u32[]{:S(2)}, u32[]{:S(2)}) collective-permute-start(bf16[16,16,128]{2,1,0:T(8,128)(2,1)} %get-tuple-element.223), channel_id=1, source_target_pairs={{0,2},{1,3},{2,4},{3,5},{4,6},{5,7},{6,8},{7,9},{8,10},{9,11},{10,... | collective-permute-start | bytes 196616 | tf_op jit(solution)/shard_map/while/body/eval_jaxpr/ppermute | solution.py:480
  57.2 4.3 %collective-permute-start = (bf16[16,16,128]{2,1,0:T(8,128)(2,1)}, bf16[16,16,128]{2,1,0:T(8,128)(2,1)S(1)}, u32[]{:S(2)}, u32[]{:S(2)}) collective-permute-start(bf16[16,16,128]{2,1,0:T(8,128)(2,1)} %get-tuple-element.223), channel_id=1, source_target_pairs={{0,3},{1,4},{2,5},{3,6},{4,7},{5,8},{6,9},{7,10},{8,11},{9,12},{10... | collective-permute-start | bytes 196616 | tf_op jit(solution)/shard_map/while/body/eval_jaxpr/ppermute | solution.py:480
  61.6 0.0 collective-permute-done.2
  61.6 0.0 collective-permute-done.1
  61.6 2.2 %collective-permute-done = bf16[16,16,128]{2,1,0:T(8,128)(2,1)S(1)} collective-permute-done((bf16[16,16,128]{2,1,0:T(8,128)(2,1)}, bf16[16,16,128]{2,1,0:T(8,128)(2,1)S(1)}, u32[]{:S(2)}, u32[]{:S(2)}) %collective-permute-start) | collective-permute-done | bytes 65568 | tf_op jit(solution)/shard_map/while/body/eval_jaxpr/ppermute | solution.py:480
  63.8 0.9 add_convert_fusion.2
  64.7 3.5 %collective-permute-start.5 = (bf16[16,16,128]{2,1,0:T(8,128)(2,1)S(1)}, bf16[16,16,128]{2,1,0:T(8,128)(2,1)S(1)}, u32[]{:S(2)}, u32[]{:S(2)}) collective-permute-start(bf16[16,16,128]{2,1,0:T(8,128)(2,1)S(1)} %add_convert_fusion.2), channel_id=1, source_target_pairs={{0,4},{1,5},{2,6},{3,7},{4,8},{5,9},{6,10},{7,11},{8,12},{9,13},{1... | collective-permute-start | bytes 196616 | tf_op jit(solution)/shard_map/while/body/eval_jaxpr/ppermute | solution.py:480
  68.2 3.7 %collective-permute-start.4 = (bf16[16,16,128]{2,1,0:T(8,128)(2,1)S(1)}, bf16[16,16,128]{2,1,0:T(8,128)(2,1)S(1)}, u32[]{:S(2)}, u32[]{:S(2)}) collective-permute-start(bf16[16,16,128]{2,1,0:T(8,128)(2,1)S(1)} %add_convert_fusion.2), channel_id=1, source_target_pairs={{0,8},{1,9},{2,10},{3,11},{4,12},{5,13},{6,14},{7,15},{16,24},{17,... | collective-permute-start | bytes 196616 | tf_op jit(solution)/shard_map/while/body/eval_jaxpr/ppermute | solution.py:480
  71.9 1.3 collective-permute-start.3
  73.2 0.0 collective-permute-done.5
  73.2 1.0 collective-permute-done.4
  74.3 1.4 collective-permute-done.3
  75.7 1.7 %fusion.2 = (f32[16,16,128]{2,1,0:T(8,128)}, f32[16,16,128]{2,1,0:T(8,128)S(1)}) fusion(f32[16,16,128]{2,1,0:T(8,128)} %get-tuple-element.222, bf16[16,16,128]{2,1,0:T(8,128)(2,1)S(1)} %collective-permute-done.3, bf16[16,16,128]{2,1,0:T(8,128)(2,1)S(1)} %collective-permute-done.4, bf16[16,16,128]{2,1,0:T(8,128)(2,1)S(1)} %collective-permute-done.5, ...), kind=kLoop, calls=%fused_computation.4.clone.1 | loop fusion | flops 425984 | bytes 917505 | tf_op jit(solution)/shard_map/while/body/eval_jaxpr/add | solution.py:522
  77.4 48.8 %denoise.1 = (f32[16,16,128]{2,1,0:T(8,128)}, bf16[16,16,128]{2,1,0:T(8,128)(2,1)}) custom-call(s32[1]{0:T(128)} %get-tuple-element.264.timestep, f32[16]{0:T(128)} %get-tuple-element.265.rate_state, f32[16]{0:T(128)} %get-tuple-element.266.rate_denoise, f32[16]{0:T(128)} %get-tuple-element.267.rate_noise, f32[16,16,128]{2,1,0:T(8,128)S(1)} %get-tuple-element.244.latent, ...), custom_call_target="tpu_custom_call" | custom-call | tf_op jit(solution)/shard_map/while/body/eval_jaxpr/denoise/pallas_call | solution.py:392
  126.2 1.9 %collective-permute-start.2 = (bf16[16,16,128]{2,1,0:T(8,128)(2,1)}, bf16[16,16,128]{2,1,0:T(8,128)(2,1)S(1)}, u32[]{:S(2)}, u32[]{:S(2)}) collective-permute-start(bf16[16,16,128]{2,1,0:T(8,128)(2,1)} %get-tuple-element.223), channel_id=1, source_target_pairs={{0,1},{1,2},{2,3},{3,4},{4,5},{5,6},{6,7},{7,8},{8,9},{9,10},{10,1... | collective-permute-start | bytes 196616 | tf_op jit(solution)/shard_map/while/body/eval_jaxpr/ppermute | solution.py:480
  128.2 2.6 %collective-permute-start.1 = (bf16[16,16,128]{2,1,0:T(8,128)(2,1)}, bf16[16,16,128]{2,1,0:T(8,128)(2,1)S(1)}, u32[]{:S(2)}, u32[]{:S(2)}) collective-permute-start(bf16[16,16,128]{2,1,0:T(8,128)(2,1)} %get-tuple-element.223), channel_id=1, source_target_pairs={{0,2},{1,3},{2,4},{3,5},{4,6},{5,7},{6,8},{7,9},{8,10},{9,11},{10,... | collective-permute-start | bytes 196616 | tf_op jit(solution)/shard_map/while/body/eval_jaxpr/ppermute | solution.py:480
  130.8 1.3 collective-permute-start
  132.1 0.0 collective-permute-done.2
  132.1 0.9 collective-permute-done.1
  133.0 1.3 collective-permute-done
  134.3 0.9 add_convert_fusion.2
  135.2 6.4 %collective-permute-start.5 = (bf16[16,16,128]{2,1,0:T(8,128)(2,1)S(1)}, bf16[16,16,128]{2,1,0:T(8,128)(2,1)S(1)}, u32[]{:S(2)}, u32[]{:S(2)}) collective-permute-start(bf16[16,16,128]{2,1,0:T(8,128)(2,1)S(1)} %add_convert_fusion.2), channel_id=1, source_target_pairs={{0,4},{1,5},{2,6},{3,7},{4,8},{5,9},{6,10},{7,11},{8,12},{9,13},{1... | collective-permute-start | bytes 196616 | tf_op jit(solution)/shard_map/while/body/eval_jaxpr/ppermute | solution.py:480
  141.7 5.0 %collective-permute-start.4 = (bf16[16,16,128]{2,1,0:T(8,128)(2,1)S(1)}, bf16[16,16,128]{2,1,0:T(8,128)(2,1)S(1)}, u32[]{:S(2)}, u32[]{:S(2)}) collective-permute-start(bf16[16,16,128]{2,1,0:T(8,128)(2,1)S(1)} %add_convert_fusion.2), channel_id=1, source_target_pairs={{0,8},{1,9},{2,10},{3,11},{4,12},{5,13},{6,14},{7,15},{16,24},{17,... | collective-permute-start | bytes 196616 | tf_op jit(solution)/shard_map/while/body/eval_jaxpr/ppermute | solution.py:480
  146.6 1.3 collective-permute-start.3
  147.9 0.0 collective-permute-done.5
  147.9 1.1 collective-permute-done.4
  149.1 1.4 collective-permute-done.3
  150.5 1.7 %fusion.2 = (f32[16,16,128]{2,1,0:T(8,128)}, f32[16,16,128]{2,1,0:T(8,128)S(1)}) fusion(f32[16,16,128]{2,1,0:T(8,128)} %get-tuple-element.222, bf16[16,16,128]{2,1,0:T(8,128)(2,1)S(1)} %collective-permute-done.3, bf16[16,16,128]{2,1,0:T(8,128)(2,1)S(1)} %collective-permute-done.4, bf16[16,16,128]{2,1,0:T(8,128)(2,1)S(1)} %collective-permute-done.5, ...), kind=kLoop, calls=%fused_computation.4.clone.1 | loop fusion | flops 425984 | bytes 917505 | tf_op jit(solution)/shard_map/while/body/eval_jaxpr/add | solution.py:522
Async XLA Ops:
  50.4 11.2 %collective-permute-start.2 = (bf16[16,16,128]{2,1,0:T(8,128)(2,1)}, bf16[16,16,128]{2,1,0:T(8,128)(2,1)S(1)}, u32[]{:S(2)}, u32[]{:S(2)}) collective-permute-start(bf16[16,16,128]{2,1,0:T(8,128)(2,1)} %get-tuple-element.223), channel_id=1, source_target_pairs={{0,1},{1,2},{2,3},{3,4},{4,5},{5,6},{6,7},{7,8},{8,9},{9,10},{10,1... | collective-permute-start | bytes 196616 | tf_op jit(solution)/shard_map/while/body/eval_jaxpr/ppermute | solution.py:480
  52.8 8.8 %collective-permute-start.1 = (bf16[16,16,128]{2,1,0:T(8,128)(2,1)}, bf16[16,16,128]{2,1,0:T(8,128)(2,1)S(1)}, u32[]{:S(2)}, u32[]{:S(2)}) collective-permute-start(bf16[16,16,128]{2,1,0:T(8,128)(2,1)} %get-tuple-element.223), channel_id=1, source_target_pairs={{0,2},{1,3},{2,4},{3,5},{4,6},{5,7},{6,8},{7,9},{8,10},{9,11},{10,... | collective-permute-start | bytes 196616 | tf_op jit(solution)/shard_map/while/body/eval_jaxpr/ppermute | solution.py:480
  57.2 6.5 %collective-permute-start = (bf16[16,16,128]{2,1,0:T(8,128)(2,1)}, bf16[16,16,128]{2,1,0:T(8,128)(2,1)S(1)}, u32[]{:S(2)}, u32[]{:S(2)}) collective-permute-start(bf16[16,16,128]{2,1,0:T(8,128)(2,1)} %get-tuple-element.223), channel_id=1, source_target_pairs={{0,3},{1,4},{2,5},{3,6},{4,7},{5,8},{6,9},{7,10},{8,11},{9,12},{10... | collective-permute-start | bytes 196616 | tf_op jit(solution)/shard_map/while/body/eval_jaxpr/ppermute | solution.py:480
  64.7 8.5 %collective-permute-start.5 = (bf16[16,16,128]{2,1,0:T(8,128)(2,1)S(1)}, bf16[16,16,128]{2,1,0:T(8,128)(2,1)S(1)}, u32[]{:S(2)}, u32[]{:S(2)}) collective-permute-start(bf16[16,16,128]{2,1,0:T(8,128)(2,1)S(1)} %add_convert_fusion.2), channel_id=1, source_target_pairs={{0,4},{1,5},{2,6},{3,7},{4,8},{5,9},{6,10},{7,11},{8,12},{9,13},{1... | collective-permute-start | bytes 196616 | tf_op jit(solution)/shard_map/while/body/eval_jaxpr/ppermute | solution.py:480
  68.2 6.0 %collective-permute-start.4 = (bf16[16,16,128]{2,1,0:T(8,128)(2,1)S(1)}, bf16[16,16,128]{2,1,0:T(8,128)(2,1)S(1)}, u32[]{:S(2)}, u32[]{:S(2)}) collective-permute-start(bf16[16,16,128]{2,1,0:T(8,128)(2,1)S(1)} %add_convert_fusion.2), channel_id=1, source_target_pairs={{0,8},{1,9},{2,10},{3,11},{4,12},{5,13},{6,14},{7,15},{16,24},{17,... | collective-permute-start | bytes 196616 | tf_op jit(solution)/shard_map/while/body/eval_jaxpr/ppermute | solution.py:480
  71.9 3.8 %collective-permute-start.3 = (bf16[16,16,128]{2,1,0:T(8,128)(2,1)S(1)}, bf16[16,16,128]{2,1,0:T(8,128)(2,1)S(1)}, u32[]{:S(2)}, u32[]{:S(2)}) collective-permute-start(bf16[16,16,128]{2,1,0:T(8,128)(2,1)S(1)} %add_convert_fusion.2), channel_id=1, source_target_pairs={{0,12},{1,13},{2,14},{3,15},{16,28},{17,29},{18,30},{19,31}} | collective-permute-start | bytes 196616 | tf_op jit(solution)/shard_map/while/body/eval_jaxpr/ppermute | solution.py:480
  126.2 5.9 %collective-permute-start.2 = (bf16[16,16,128]{2,1,0:T(8,128)(2,1)}, bf16[16,16,128]{2,1,0:T(8,128)(2,1)S(1)}, u32[]{:S(2)}, u32[]{:S(2)}) collective-permute-start(bf16[16,16,128]{2,1,0:T(8,128)(2,1)} %get-tuple-element.223), channel_id=1, source_target_pairs={{0,1},{1,2},{2,3},{3,4},{4,5},{5,6},{6,7},{7,8},{8,9},{9,10},{10,1... | collective-permute-start | bytes 196616 | tf_op jit(solution)/shard_map/while/body/eval_jaxpr/ppermute | solution.py:480
  128.2 4.8 %collective-permute-start.1 = (bf16[16,16,128]{2,1,0:T(8,128)(2,1)}, bf16[16,16,128]{2,1,0:T(8,128)(2,1)S(1)}, u32[]{:S(2)}, u32[]{:S(2)}) collective-permute-start(bf16[16,16,128]{2,1,0:T(8,128)(2,1)} %get-tuple-element.223), channel_id=1, source_target_pairs={{0,2},{1,3},{2,4},{3,5},{4,6},{5,7},{6,8},{7,9},{8,10},{9,11},{10,... | collective-permute-start | bytes 196616 | tf_op jit(solution)/shard_map/while/body/eval_jaxpr/ppermute | solution.py:480
  130.8 3.5 %collective-permute-start = (bf16[16,16,128]{2,1,0:T(8,128)(2,1)}, bf16[16,16,128]{2,1,0:T(8,128)(2,1)S(1)}, u32[]{:S(2)}, u32[]{:S(2)}) collective-permute-start(bf16[16,16,128]{2,1,0:T(8,128)(2,1)} %get-tuple-element.223), channel_id=1, source_target_pairs={{0,3},{1,4},{2,5},{3,6},{4,7},{5,8},{6,9},{7,10},{8,11},{9,12},{10... | collective-permute-start | bytes 196616 | tf_op jit(solution)/shard_map/while/body/eval_jaxpr/ppermute | solution.py:480
  135.2 12.7 %collective-permute-start.5 = (bf16[16,16,128]{2,1,0:T(8,128)(2,1)S(1)}, bf16[16,16,128]{2,1,0:T(8,128)(2,1)S(1)}, u32[]{:S(2)}, u32[]{:S(2)}) collective-permute-start(bf16[16,16,128]{2,1,0:T(8,128)(2,1)S(1)} %add_convert_fusion.2), channel_id=1, source_target_pairs={{0,4},{1,5},{2,6},{3,7},{4,8},{5,9},{6,10},{7,11},{8,12},{9,13},{1... | collective-permute-start | bytes 196616 | tf_op jit(solution)/shard_map/while/body/eval_jaxpr/ppermute | solution.py:480
  141.7 7.4 %collective-permute-start.4 = (bf16[16,16,128]{2,1,0:T(8,128)(2,1)S(1)}, bf16[16,16,128]{2,1,0:T(8,128)(2,1)S(1)}, u32[]{:S(2)}, u32[]{:S(2)}) collective-permute-start(bf16[16,16,128]{2,1,0:T(8,128)(2,1)S(1)} %add_convert_fusion.2), channel_id=1, source_target_pairs={{0,8},{1,9},{2,10},{3,11},{4,12},{5,13},{6,14},{7,15},{16,24},{17,... | collective-permute-start | bytes 196616 | tf_op jit(solution)/shard_map/while/body/eval_jaxpr/ppermute | solution.py:480
  146.6 3.8 %collective-permute-start.3 = (bf16[16,16,128]{2,1,0:T(8,128)(2,1)S(1)}, bf16[16,16,128]{2,1,0:T(8,128)(2,1)S(1)}, u32[]{:S(2)}, u32[]{:S(2)}) collective-permute-start(bf16[16,16,128]{2,1,0:T(8,128)(2,1)S(1)} %add_convert_fusion.2), channel_id=1, source_target_pairs={{0,12},{1,13},{2,14},{3,15},{16,28},{17,29},{18,30},{19,31}} | collective-permute-start | bytes 196616 | tf_op jit(solution)/shard_map/while/body/eval_jaxpr/ppermute | solution.py:480
where the time goes:
time: 153 us; the launch traced here: 152 us
  Pallas kernels  97.7 us (64%)
  starting transfers between devices  38.2 us (25%)
  waiting for transfers between devices  9.35 us (6%)
  other arithmetic  5.22 us (3%)
  local copies, waits for them, and re-layouts  1.56 us (1%)
    pallas_call x2, Pallas kernels, step_fused(): pl.pallas_call(fused_kernel, out_shape=[jax.ShapeDtypeStruct(latent.shape...  97.7 us
    ppermute x12, starting transfers between devices, sum_before(): arrived.append(lax.ppermute(held, 'tok', moves))  38.2 us
    ppermute x12, waiting for transfers between devices, sum_before(): arrived.append(lax.ppermute(held, 'tok', moves))  9.35 us
    add x2, other arithmetic, iterate(): return (jnp.where(leading, latent, before), before + increment)  3.34 us
  transfers between devices with their start and end apart: 12, of which 7 were waited for; matrix products, arithmetic and copies ran while one was open for 0% of the time, Pallas kernels for 0%

commit v1 on v0

--- a/solution.py
+++ b/solution.py
@@ -201,7 +201,7 @@
     width = embed.shape[1]
     step = groups_of(frames)
     tokens = step * spatial
-    normed, base, inner_places = places[:2], places[2:4], places[4:]
+    normed, base, inner_places = places[:2], places[2:4], places[5:]
     groups = [slice(at, at + spatial) for at in range(0, tokens, spatial)]
 
     def before(index, own):
@@ -242,7 +242,7 @@
     step = groups_of(positions // ROWS8)
     rows = frames * ROWS8
     tokens = step * rows
-    normed, settled, inner_places = places[:2], places[2:4], places[4:]
+    normed, settled, last, inner_places = places[:2], places[2:4], places[4], places[5:]
     groups = [slice(at, at + rows) for at in range(0, tokens, rows)]
     same_position = same_position_mask(frames, min(step, 2))
 
@@ -274,23 +274,21 @@
         )
 
     def behind(index, own):
+        for at in range(0, tokens, BLOCK):
+            last[at : at + BLOCK] = modulated_norm(settled[own][at : at + BLOCK], rows_of, 6, 7)
+            yield
+        predicted = lax.dot_general(
+            final[...], last[...], (((1,), (1,)), ((), ())), preferred_element_type=F32
+        )
         for group in range(step):
-            for at in range(0, rows, BLOCK):
-                first = groups[group].start + at
-                last = modulated_norm(settled[own][first : first + BLOCK], rows_of, 6, 7)
-                predicted = lax.dot_general(
-                    last, final[...], (((1,), (1,)), ((), ())), preferred_element_type=F32
-                )
-                some = slice(at // ROWS8, (at + BLOCK) // ROWS8)
-                out[some, eight(index, group), :] = predicted.reshape(
-                    BLOCK // ROWS8, ROWS8, predicted.shape[1]
-                )
-                yield
+            part = predicted[:, groups[group]].T
+            out[:, eight(index, group), :] = part.reshape(frames, ROWS8, part.shape[1])
+        yield
 
     settled[1][...] = jnp.zeros_like(settled[1])
     run_pipelined(
         positions // (step * ROWS8), before, main, behind, main_pieces(step, width),
-        tokens // BLOCK, tokens // BLOCK, ready,
+        tokens // BLOCK, tokens // BLOCK + 1, ready,
     )
 
 
@@ -372,6 +370,7 @@
         pltpu.VMEM((tokens, width), BF16),
         pltpu.VMEM((tokens, width), F32),
         pltpu.VMEM((tokens, width), F32),
+        pltpu.VMEM((tokens, width), BF16),
         pltpu.VMEM((HEADS, deep, tokens), BF16),
         pltpu.VMEM((HEADS, tokens, deep), BF16),
         pltpu.VMEM((HEADS, tall, tokens), BF16),
@@ -463,26 +462,32 @@
     return increment, increment.astype(BF16)
 
 
-RADIX = 4
-
-
-def sum_before(values, held, timesteps, groups):
-    before = jnp.zeros_like(values)
-    reach = 1
-    while reach < timesteps:
-        arrived = []
-        for back in range(reach, min(reach * RADIX, timesteps), reach):
-            moves = [
-                (step * groups + block, (step + back) * groups + block)
-                for step in range(timesteps - back)
-                for block in range(groups)
-            ]
-            arrived.append(lax.ppermute(held, "tok", moves))
-        for part in arrived:
-            before = before + part.astype(F32)
-        held = (values + before).astype(BF16)
-        reach *= RADIX
-    return before
+def earlier_kernel(parts, sums):
+    total = jnp.zeros(parts.shape[1:], F32)
+    for step in range(parts.shape[0]):
+        sums[step] = total.astype(BF16)
+        total = total + parts[step].astype(F32)
+
+
+def sum_before(held, timesteps, groups):
+    frames, channels, spatial = held.shape
+    rows = frames * channels
+    peers = None
+    if groups > 1:
+        peers = [[step * groups + block for step in range(timesteps)] for block in range(groups)]
+    swap = functools.partial(
+        lax.all_to_all, axis_name="tok", split_axis=0, concat_axis=0, tiled=True,
+        axis_index_groups=peers,
+    )
+    parts = swap(held.reshape(rows, spatial)).reshape(timesteps, rows // timesteps, spatial)
+    sums = pl.pallas_call(
+        earlier_kernel,
+        out_shape=jax.ShapeDtypeStruct(parts.shape, BF16),
+        in_specs=vmem(1),
+        out_specs=vmem(1)[0],
+        name="earlier",
+    )(parts)
+    return swap(sums.reshape(rows, spatial)).reshape(held.shape).astype(F32)
 
 
 def body(
@@ -518,7 +523,7 @@
     def iterate(_, held):
         latent = held[0]
         increment, rounded = step(own, rates, latent, noise_draws, modulation, weights)
-        before = sum_before(increment, rounded, timesteps, groups)
+        before = sum_before(rounded, timesteps, groups)
         return jnp.where(leading, latent, before), before + increment
 
     return lax.fori_loop(0, ITERS, iterate, (initial_guess, initial_guess))[1]

time: 153 us -> 152 us (level)
  starting transfers between devices: 38.2 us -> 6.98 us
  blocking collectives: 0 us -> 25.4 us
  waiting for transfers between devices: 9.35 us -> 13.7 us
  Pallas kernels: 97.7 us -> 101 us
  other arithmetic: 5.22 us -> 3.21 us
    ppermute x12 -> x0, starting transfers between devices: 38.2 us -> none  [sum_before(): arrived.append(lax.ppermute(held, 'tok', moves))]
    all_to_all x0 -> x2, blocking collectives: none -> 25.4 us  [sum_before(): swap(held.reshape(rows, spatial))]
    all_to_all x0 -> x2, waiting for transfers between devices: none -> 13.7 us  [sum_before(): return swap(sums.reshape(rows, spatial)).reshape(held.shape).astype(F32)]
    ppermute x12 -> x0, waiting for transfers between devices: 9.35 us -> none  [sum_before(): arrived.append(lax.ppermute(held, 'tok', moves))]
    all_to_all x0 -> x2, starting transfers between devices: none -> 6.98 us  [sum_before(): return swap(sums.reshape(rows, spatial)).reshape(held.shape).astype(F32)]
    pallas_call x0 -> x2, Pallas kernels: none -> 2.95 us  [sum_before(): pl.pallas_call(earlier_kernel, out_shape=jax.ShapeDtypeStruct(parts.shape...]
    convert_element_type x2 -> x0, other arithmetic: 1.87 us -> none  [sum_before(): held = (values + before).astype(BF16)]
  transfers between devices with their start and end apart: 12 -> 2, of which waited for: 7 -> 2; matrix products, arithmetic and copies ran while one was open for 0% -> 0% of each run, Pallas kernels for 0% -> 0%
where the time goes in v1:
time: 152 us
  Pallas kernels  101 us (66%)
  blocking collectives  25.4 us (17%)
  waiting for transfers between devices  13.7 us (9%)
  starting transfers between devices  6.98 us (5%)
  other arithmetic  3.21 us (2%)
  local copies, waits for them, and re-layouts  1.56 us (1%)
    pallas_call x2, Pallas kernels, step_fused(): pl.pallas_call(fused_kernel, out_shape=[jax.ShapeDtypeStruct(latent.shape...  97.7 us
    all_to_all x2, blocking collectives, sum_before(): swap(held.reshape(rows, spatial))  25.4 us
    all_to_all x2, waiting for transfers between devices, sum_before(): return swap(sums.reshape(rows, spatial)).reshape(held.shape).astype(F32)  13.7 us
    all_to_all x2, starting transfers between devices, sum_before(): return swap(sums.reshape(rows, spatial)).reshape(held.shape).astype(F32)  6.98 us
    add x2, other arithmetic, iterate(): return (jnp.where(leading, latent, before), before + increment)  3.21 us
  transfers between devices with their start and end apart: 2, of which 2 were waited for; matrix products, arithmetic and copies ran while one was open for 0% of the time, Pallas kernels for 0%

profile of v1, /device:TPU:0, one launch (start us, length us, event | category | flops | bytes accessed | tf_op | source)
XLA Modules:
  0.0 151.6 jit_solution(2981978569585976349)
XLA Ops:
  0.0 0.9 copy.24
  0.9 0.7 copy.15
  1.6 150.0 %while.12 = (s32[]{:T(128)}, f32[16,16,128]{2,1,0:T(8,128)S(1)}, f32[16,16,128]{2,1,0:T(8,128)}, pred[]{:T(512)}, s32[1]{0:T(128)}, /*index=5*/f32[16]{0:T(128)}...) while((s32[]{:T(128)}, f32[16,16,128]{2,1,0:T(8,128)S(1)}, ...), condition=%wide.region_1.2_spmd, body=%wide.region_0.1_spmd.sunk | while | flops 98306 | bytes 917694 | solution.py:529
  1.6 48.9 %denoise.1 = (f32[16,16,128]{2,1,0:T(8,128)}, bf16[16,16,128]{2,1,0:T(8,128)(2,1)}) custom-call(s32[1]{0:T(128)} %get-tuple-element.264.timestep, f32[16]{0:T(128)} %get-tuple-element.265.rate_state, f32[16]{0:T(128)} %get-tuple-element.266.rate_denoise, f32[16]{0:T(128)} %get-tuple-element.267.rate_noise, f32[16,16,128]{2,1,0:T(8,128)S(1)} %get-tuple-element.244.latent, ...), custom_call_target="tpu_custom_call" | custom-call | tf_op jit(solution)/shard_map/while/body/eval_jaxpr/denoise/pallas_call | solution.py:391
  50.4 14.4 %all_to_all.14.parts = bf16[16,16,128]{2,1,0:T(8,128)(2,1)} all-to-all(bf16[16,16,128]{2,1,0:T(8,128)(2,1)} %get-tuple-element.223), channel_id=1, replica_groups=mesh['group'=2,'tok'=16] {'tok'}, dimensions={0} | all-to-all | bytes 131072 | tf_op jit(solution)/shard_map/while/body/eval_jaxpr/all_to_all | solution.py:482
  64.8 1.5 earlier.1
  66.3 3.5 %all-to-all-start.1 = ((bf16[16,16,128]{2,1,0:T(8,128)(2,1)}), bf16[16,16,128]{2,1,0:T(8,128)(2,1)S(1)}, u32[]{:S(2)}, u32[]{:S(2)}) async-start(bf16[16,16,128]{2,1,0:T(8,128)(2,1)} %earlier.1), calls=%async_computation.1 | async-start | bytes 131072 | tf_op jit(solution)/shard_map/while/body/eval_jaxpr/all_to_all | solution.py:490
  69.8 6.9 %all-to-all-done.1 = bf16[16,16,128]{2,1,0:T(8,128)(2,1)S(1)} async-done(((bf16[16,16,128]{2,1,0:T(8,128)(2,1)}), bf16[16,16,128]{2,1,0:T(8,128)(2,1)S(1)}, u32[]{:S(2)}, u32[]{:S(2)}) %all-to-all-start.1) | async-done | bytes 65568 | tf_op jit(solution)/shard_map/while/body/eval_jaxpr/all_to_all | solution.py:490
  76.6 1.6 %convert_add_fusion.2 = (f32[16,16,128]{2,1,0:T(8,128)}, f32[16,16,128]{2,1,0:T(8,128)S(1)}) fusion(f32[16,16,128]{2,1,0:T(8,128)} %get-tuple-element.222, bf16[16,16,128]{2,1,0:T(8,128)(2,1)S(1)} %all-to-all-done.1, f32[16,16,128]{2,1,0:T(8,128)S(1)} %get-tuple-element.244.latent, pred[]{:T(512)} %get-tuple-element.263), kind=kLoop, calls=%fused_computation.clone.1 | loop fusion | flops 98304 | bytes 589825 | tf_op jit(solution)/shard_map/while/body/eval_jaxpr/add | solution.py:527
  78.3 48.8 %denoise.1 = (f32[16,16,128]{2,1,0:T(8,128)}, bf16[16,16,128]{2,1,0:T(8,128)(2,1)}) custom-call(s32[1]{0:T(128)} %get-tuple-element.264.timestep, f32[16]{0:T(128)} %get-tuple-element.265.rate_state, f32[16]{0:T(128)} %get-tuple-element.266.rate_denoise, f32[16]{0:T(128)} %get-tuple-element.267.rate_noise, f32[16,16,128]{2,1,0:T(8,128)S(1)} %get-tuple-element.244.latent, ...), custom_call_target="tpu_custom_call" | custom-call | tf_op jit(solution)/shard_map/while/body/eval_jaxpr/denoise/pallas_call | solution.py:391
  127.1 11.1 %all_to_all.14.parts = bf16[16,16,128]{2,1,0:T(8,128)(2,1)} all-to-all(bf16[16,16,128]{2,1,0:T(8,128)(2,1)} %get-tuple-element.223), channel_id=1, replica_groups=mesh['group'=2,'tok'=16] {'tok'}, dimensions={0} | all-to-all | bytes 131072 | tf_op jit(solution)/shard_map/while/body/eval_jaxpr/all_to_all | solution.py:482
  138.2 1.5 earlier.1
  139.6 3.5 %all-to-all-start.1 = ((bf16[16,16,128]{2,1,0:T(8,128)(2,1)}), bf16[16,16,128]{2,1,0:T(8,128)(2,1)S(1)}, u32[]{:S(2)}, u32[]{:S(2)}) async-start(bf16[16,16,128]{2,1,0:T(8,128)(2,1)} %earlier.1), calls=%async_computation.1 | async-start | bytes 131072 | tf_op jit(solution)/shard_map/while/body/eval_jaxpr/all_to_all | solution.py:490
  143.1 6.9 %all-to-all-done.1 = bf16[16,16,128]{2,1,0:T(8,128)(2,1)S(1)} async-done(((bf16[16,16,128]{2,1,0:T(8,128)(2,1)}), bf16[16,16,128]{2,1,0:T(8,128)(2,1)S(1)}, u32[]{:S(2)}, u32[]{:S(2)}) %all-to-all-start.1) | async-done | bytes 65568 | tf_op jit(solution)/shard_map/while/body/eval_jaxpr/all_to_all | solution.py:490
  150.0 1.6 %convert_add_fusion.2 = (f32[16,16,128]{2,1,0:T(8,128)}, f32[16,16,128]{2,1,0:T(8,128)S(1)}) fusion(f32[16,16,128]{2,1,0:T(8,128)} %get-tuple-element.222, bf16[16,16,128]{2,1,0:T(8,128)(2,1)S(1)} %all-to-all-done.1, f32[16,16,128]{2,1,0:T(8,128)S(1)} %get-tuple-element.244.latent, pred[]{:T(512)} %get-tuple-element.263), kind=kLoop, calls=%fused_computation.clone.1 | loop fusion | flops 98304 | bytes 589825 | tf_op jit(solution)/shard_map/while/body/eval_jaxpr/add | solution.py:527
Async XLA Ops:
  66.3 10.4 %all-to-all-start.1 = ((bf16[16,16,128]{2,1,0:T(8,128)(2,1)}), bf16[16,16,128]{2,1,0:T(8,128)(2,1)S(1)}, u32[]{:S(2)}, u32[]{:S(2)}) async-start(bf16[16,16,128]{2,1,0:T(8,128)(2,1)} %earlier.1), calls=%async_computation.1 | async-start | bytes 131072 | tf_op jit(solution)/shard_map/while/body/eval_jaxpr/all_to_all | solution.py:490
  139.6 10.4 %all-to-all-start.1 = ((bf16[16,16,128]{2,1,0:T(8,128)(2,1)}), bf16[16,16,128]{2,1,0:T(8,128)(2,1)S(1)}, u32[]{:S(2)}, u32[]{:S(2)}) async-start(bf16[16,16,128]{2,1,0:T(8,128)(2,1)} %earlier.1), calls=%async_computation.1 | async-start | bytes 131072 | tf_op jit(solution)/shard_map/while/body/eval_jaxpr/all_to_all | solution.py:490

commit v2 on v0

--- a/solution.py
+++ b/solution.py
@@ -72,15 +72,19 @@
     chunk = HEADS // 2
     scale = head_size ** (-0.5) * math.log2(math.e)
 
-    def project(kind):
-        rows = input_turned[kind * inner : (kind + 1) * inner]
+    half_heads = HEADS // 2
+
+    def project(kind, half):
+        at = kind * inner + half * half_heads * head_size
+        rows = input_turned[at : at + half_heads * head_size]
         return lax.dot_general(
             rows, normed[...], (((1,), (1,)), ((), ())), preferred_element_type=F32
         )
 
-    def keep_projected(kind, packed):
-        for head in range(HEADS):
-            values = packed[head * head_size : (head + 1) * head_size]
+    def keep_projected(kind, half, packed):
+        for index in range(half_heads):
+            head = half * half_heads + index
+            values = packed[index * head_size : (index + 1) * head_size]
             if kind == 0:
                 query_rows[head] = padded(normed_head(values, head_size, scale), 0.0, deep)
             elif kind == 1:
@@ -124,8 +128,8 @@
             if first < stop <= last:
                 turned_attended[columns, at:stop] = attended[at:stop, columns].astype(BF16).T
 
-    def projections(kind):
-        return (lambda: project(kind)), (lambda got: keep_projected(kind, got))
+    def projections(kind, half):
+        return (lambda: project(kind, half)), (lambda got: keep_projected(kind, half, got))
 
     def scorings(head, pair):
         return (lambda: score(head, pair)), (lambda got: keep_scored(head, pair, got))
@@ -144,8 +148,10 @@
     every = [(head, pair) for head in range(HEADS) for pair in pairs]
     scored = [scorings(*at) for at in every]
     mixes = [mixings(*at) for at in every]
-    first = [projections(0), projections(1), projections(2), scored[0]]
-    behind = scored[1:]
+    first = [projections(0, 0), projections(1, 0), projections(0, 1)]
+    for task, later in zip(scored, (projections(1, 1), projections(2, 0), projections(2, 1))):
+        first += [task, later]
+    behind = scored[3:]
     for index, task in enumerate(behind):
         first.append(task)
         if index >= 1:
@@ -164,7 +170,7 @@
 
 
 def main_pieces(groups, width):
-    return 3 + HEADS * -(-groups // 2) * 2 + 1 + -(-width // (2 * LANES)) + 1
+    return 6 + HEADS * -(-groups // 2) * 2 + 1 + -(-width // (2 * LANES)) + 1
 
 
 def run_pipelined(steps, before, main, behind, main_count, before_count, behind_count, ready):

time: 153 us -> 154 us (level)
  Pallas kernels: 97.7 us -> 99.5 us
    pallas_call x2, Pallas kernels: 97.7 us -> 99.5 us  [step_fused(): pl.pallas_call(fused_kernel, out_shape=[jax.ShapeDtypeStruct(latent.shape...]
where the time goes in v2:
time: 154 us
  Pallas kernels  99.5 us (65%)
  starting transfers between devices  38.2 us (25%)
  waiting for transfers between devices  9.35 us (6%)
  other arithmetic  5.22 us (3%)
  local copies, waits for them, and re-layouts  1.56 us (1%)
    pallas_call x2, Pallas kernels, step_fused(): pl.pallas_call(fused_kernel, out_shape=[jax.ShapeDtypeStruct(latent.shape...  99.5 us
    ppermute x12, starting transfers between devices, sum_before(): arrived.append(lax.ppermute(held, 'tok', moves))  38.2 us
    ppermute x12, waiting for transfers between devices, sum_before(): arrived.append(lax.ppermute(held, 'tok', moves))  9.35 us
    add x2, other arithmetic, iterate(): return (jnp.where(leading, latent, before), before + increment)  3.34 us
  transfers between devices with their start and end apart: 12, of which 7 were waited for; matrix products, arithmetic and copies ran while one was open for 0% of the time, Pallas kernels for 0%

profile of v2, /device:TPU:0, one launch (start us, length us, event | category | flops | bytes accessed | tf_op | source)
XLA Modules:
  0.0 153.9 jit_solution(15141393180782277847)
XLA Ops:
  0.0 0.9 copy.24
  0.9 0.7 copy.15
  1.6 152.4 %while.12 = (s32[]{:T(128)}, f32[16,16,128]{2,1,0:T(8,128)S(1)}, f32[16,16,128]{2,1,0:T(8,128)}, pred[]{:T(512)}, s32[1]{0:T(128)}, /*index=5*/f32[16]{0:T(128)}...) while((s32[]{:T(128)}, f32[16,16,128]{2,1,0:T(8,128)S(1)}, ...), condition=%wide.region_1.2_spmd, body=%wide.region_0.1_spmd.sunk | while | flops 655362 | bytes 2883982 | solution.py:530
  1.6 49.7 %denoise.1 = (f32[16,16,128]{2,1,0:T(8,128)}, bf16[16,16,128]{2,1,0:T(8,128)(2,1)}) custom-call(s32[1]{0:T(128)} %get-tuple-element.264.timestep, f32[16]{0:T(128)} %get-tuple-element.265.rate_state, f32[16]{0:T(128)} %get-tuple-element.266.rate_denoise, f32[16]{0:T(128)} %get-tuple-element.267.rate_noise, f32[16,16,128]{2,1,0:T(8,128)S(1)} %get-tuple-element.244.latent, ...), custom_call_target="tpu_custom_call" | custom-call | tf_op jit(solution)/shard_map/while/body/eval_jaxpr/denoise/pallas_call | solution.py:398
  51.3 2.3 %collective-permute-start.2 = (bf16[16,16,128]{2,1,0:T(8,128)(2,1)}, bf16[16,16,128]{2,1,0:T(8,128)(2,1)S(1)}, u32[]{:S(2)}, u32[]{:S(2)}) collective-permute-start(bf16[16,16,128]{2,1,0:T(8,128)(2,1)} %get-tuple-element.223), channel_id=1, source_target_pairs={{0,1},{1,2},{2,3},{3,4},{4,5},{5,6},{6,7},{7,8},{8,9},{9,10},{10,1... | collective-permute-start | bytes 196616 | tf_op jit(solution)/shard_map/while/body/eval_jaxpr/ppermute | solution.py:486
  53.7 4.5 %collective-permute-start.1 = (bf16[16,16,128]{2,1,0:T(8,128)(2,1)}, bf16[16,16,128]{2,1,0:T(8,128)(2,1)S(1)}, u32[]{:S(2)}, u32[]{:S(2)}) collective-permute-start(bf16[16,16,128]{2,1,0:T(8,128)(2,1)} %get-tuple-element.223), channel_id=1, source_target_pairs={{0,2},{1,3},{2,4},{3,5},{4,6},{5,7},{6,8},{7,9},{8,10},{9,11},{10,... | collective-permute-start | bytes 196616 | tf_op jit(solution)/shard_map/while/body/eval_jaxpr/ppermute | solution.py:486
  58.1 4.4 %collective-permute-start = (bf16[16,16,128]{2,1,0:T(8,128)(2,1)}, bf16[16,16,128]{2,1,0:T(8,128)(2,1)S(1)}, u32[]{:S(2)}, u32[]{:S(2)}) collective-permute-start(bf16[16,16,128]{2,1,0:T(8,128)(2,1)} %get-tuple-element.223), channel_id=1, source_target_pairs={{0,3},{1,4},{2,5},{3,6},{4,7},{5,8},{6,9},{7,10},{8,11},{9,12},{10... | collective-permute-start | bytes 196616 | tf_op jit(solution)/shard_map/while/body/eval_jaxpr/ppermute | solution.py:486
  62.5 0.0 collective-permute-done.2
  62.5 0.0 collective-permute-done.1
  62.5 2.2 %collective-permute-done = bf16[16,16,128]{2,1,0:T(8,128)(2,1)S(1)} collective-permute-done((bf16[16,16,128]{2,1,0:T(8,128)(2,1)}, bf16[16,16,128]{2,1,0:T(8,128)(2,1)S(1)}, u32[]{:S(2)}, u32[]{:S(2)}) %collective-permute-start) | collective-permute-done | bytes 65568 | tf_op jit(solution)/shard_map/while/body/eval_jaxpr/ppermute | solution.py:486
  64.7 0.9 add_convert_fusion.2
  65.6 3.5 %collective-permute-start.5 = (bf16[16,16,128]{2,1,0:T(8,128)(2,1)S(1)}, bf16[16,16,128]{2,1,0:T(8,128)(2,1)S(1)}, u32[]{:S(2)}, u32[]{:S(2)}) collective-permute-start(bf16[16,16,128]{2,1,0:T(8,128)(2,1)S(1)} %add_convert_fusion.2), channel_id=1, source_target_pairs={{0,4},{1,5},{2,6},{3,7},{4,8},{5,9},{6,10},{7,11},{8,12},{9,13},{1... | collective-permute-start | bytes 196616 | tf_op jit(solution)/shard_map/while/body/eval_jaxpr/ppermute | solution.py:486
  69.1 3.7 %collective-permute-start.4 = (bf16[16,16,128]{2,1,0:T(8,128)(2,1)S(1)}, bf16[16,16,128]{2,1,0:T(8,128)(2,1)S(1)}, u32[]{:S(2)}, u32[]{:S(2)}) collective-permute-start(bf16[16,16,128]{2,1,0:T(8,128)(2,1)S(1)} %add_convert_fusion.2), channel_id=1, source_target_pairs={{0,8},{1,9},{2,10},{3,11},{4,12},{5,13},{6,14},{7,15},{16,24},{17,... | collective-permute-start | bytes 196616 | tf_op jit(solution)/shard_map/while/body/eval_jaxpr/ppermute | solution.py:486
  72.8 1.3 collective-permute-start.3
  74.1 0.0 collective-permute-done.5
  74.1 1.0 collective-permute-done.4
  75.2 1.4 collective-permute-done.3
  76.6 1.7 %fusion.2 = (f32[16,16,128]{2,1,0:T(8,128)}, f32[16,16,128]{2,1,0:T(8,128)S(1)}) fusion(f32[16,16,128]{2,1,0:T(8,128)} %get-tuple-element.222, bf16[16,16,128]{2,1,0:T(8,128)(2,1)S(1)} %collective-permute-done.3, bf16[16,16,128]{2,1,0:T(8,128)(2,1)S(1)} %collective-permute-done.4, bf16[16,16,128]{2,1,0:T(8,128)(2,1)S(1)} %collective-permute-done.5, ...), kind=kLoop, calls=%fused_computation.4.clone.1 | loop fusion | flops 425984 | bytes 917505 | tf_op jit(solution)/shard_map/while/body/eval_jaxpr/add | solution.py:528
  78.3 49.7 %denoise.1 = (f32[16,16,128]{2,1,0:T(8,128)}, bf16[16,16,128]{2,1,0:T(8,128)(2,1)}) custom-call(s32[1]{0:T(128)} %get-tuple-element.264.timestep, f32[16]{0:T(128)} %get-tuple-element.265.rate_state, f32[16]{0:T(128)} %get-tuple-element.266.rate_denoise, f32[16]{0:T(128)} %get-tuple-element.267.rate_noise, f32[16,16,128]{2,1,0:T(8,128)S(1)} %get-tuple-element.244.latent, ...), custom_call_target="tpu_custom_call" | custom-call | tf_op jit(solution)/shard_map/while/body/eval_jaxpr/denoise/pallas_call | solution.py:398
  128.0 1.9 %collective-permute-start.2 = (bf16[16,16,128]{2,1,0:T(8,128)(2,1)}, bf16[16,16,128]{2,1,0:T(8,128)(2,1)S(1)}, u32[]{:S(2)}, u32[]{:S(2)}) collective-permute-start(bf16[16,16,128]{2,1,0:T(8,128)(2,1)} %get-tuple-element.223), channel_id=1, source_target_pairs={{0,1},{1,2},{2,3},{3,4},{4,5},{5,6},{6,7},{7,8},{8,9},{9,10},{10,1... | collective-permute-start | bytes 196616 | tf_op jit(solution)/shard_map/while/body/eval_jaxpr/ppermute | solution.py:486
  130.0 2.7 %collective-permute-start.1 = (bf16[16,16,128]{2,1,0:T(8,128)(2,1)}, bf16[16,16,128]{2,1,0:T(8,128)(2,1)S(1)}, u32[]{:S(2)}, u32[]{:S(2)}) collective-permute-start(bf16[16,16,128]{2,1,0:T(8,128)(2,1)} %get-tuple-element.223), channel_id=1, source_target_pairs={{0,2},{1,3},{2,4},{3,5},{4,6},{5,7},{6,8},{7,9},{8,10},{9,11},{10,... | collective-permute-start | bytes 196616 | tf_op jit(solution)/shard_map/while/body/eval_jaxpr/ppermute | solution.py:486
  132.6 1.3 collective-permute-start
  133.9 0.0 collective-permute-done.2
  133.9 0.9 collective-permute-done.1
  134.8 1.3 collective-permute-done
  136.1 0.9 add_convert_fusion.2
  137.1 6.4 %collective-permute-start.5 = (bf16[16,16,128]{2,1,0:T(8,128)(2,1)S(1)}, bf16[16,16,128]{2,1,0:T(8,128)(2,1)S(1)}, u32[]{:S(2)}, u32[]{:S(2)}) collective-permute-start(bf16[16,16,128]{2,1,0:T(8,128)(2,1)S(1)} %add_convert_fusion.2), channel_id=1, source_target_pairs={{0,4},{1,5},{2,6},{3,7},{4,8},{5,9},{6,10},{7,11},{8,12},{9,13},{1... | collective-permute-start | bytes 196616 | tf_op jit(solution)/shard_map/while/body/eval_jaxpr/ppermute | solution.py:486
  143.4 5.0 %collective-permute-start.4 = (bf16[16,16,128]{2,1,0:T(8,128)(2,1)S(1)}, bf16[16,16,128]{2,1,0:T(8,128)(2,1)S(1)}, u32[]{:S(2)}, u32[]{:S(2)}) collective-permute-start(bf16[16,16,128]{2,1,0:T(8,128)(2,1)S(1)} %add_convert_fusion.2), channel_id=1, source_target_pairs={{0,8},{1,9},{2,10},{3,11},{4,12},{5,13},{6,14},{7,15},{16,24},{17,... | collective-permute-start | bytes 196616 | tf_op jit(solution)/shard_map/while/body/eval_jaxpr/ppermute | solution.py:486
  148.4 1.3 collective-permute-start.3
  149.7 0.0 collective-permute-done.5
  149.7 1.1 collective-permute-done.4
  150.8 1.4 collective-permute-done.3
  152.3 1.7 %fusion.2 = (f32[16,16,128]{2,1,0:T(8,128)}, f32[16,16,128]{2,1,0:T(8,128)S(1)}) fusion(f32[16,16,128]{2,1,0:T(8,128)} %get-tuple-element.222, bf16[16,16,128]{2,1,0:T(8,128)(2,1)S(1)} %collective-permute-done.3, bf16[16,16,128]{2,1,0:T(8,128)(2,1)S(1)} %collective-permute-done.4, bf16[16,16,128]{2,1,0:T(8,128)(2,1)S(1)} %collective-permute-done.5, ...), kind=kLoop, calls=%fused_computation.4.clone.1 | loop fusion | flops 425984 | bytes 917505 | tf_op jit(solution)/shard_map/while/body/eval_jaxpr/add | solution.py:528
Async XLA Ops:
  51.3 11.2 %collective-permute-start.2 = (bf16[16,16,128]{2,1,0:T(8,128)(2,1)}, bf16[16,16,128]{2,1,0:T(8,128)(2,1)S(1)}, u32[]{:S(2)}, u32[]{:S(2)}) collective-permute-start(bf16[16,16,128]{2,1,0:T(8,128)(2,1)} %get-tuple-element.223), channel_id=1, source_target_pairs={{0,1},{1,2},{2,3},{3,4},{4,5},{5,6},{6,7},{7,8},{8,9},{9,10},{10,1... | collective-permute-start | bytes 196616 | tf_op jit(solution)/shard_map/while/body/eval_jaxpr/ppermute | solution.py:486
  53.7 8.8 %collective-permute-start.1 = (bf16[16,16,128]{2,1,0:T(8,128)(2,1)}, bf16[16,16,128]{2,1,0:T(8,128)(2,1)S(1)}, u32[]{:S(2)}, u32[]{:S(2)}) collective-permute-start(bf16[16,16,128]{2,1,0:T(8,128)(2,1)} %get-tuple-element.223), channel_id=1, source_target_pairs={{0,2},{1,3},{2,4},{3,5},{4,6},{5,7},{6,8},{7,9},{8,10},{9,11},{10,... | collective-permute-start | bytes 196616 | tf_op jit(solution)/shard_map/while/body/eval_jaxpr/ppermute | solution.py:486
  58.1 6.6 %collective-permute-start = (bf16[16,16,128]{2,1,0:T(8,128)(2,1)}, bf16[16,16,128]{2,1,0:T(8,128)(2,1)S(1)}, u32[]{:S(2)}, u32[]{:S(2)}) collective-permute-start(bf16[16,16,128]{2,1,0:T(8,128)(2,1)} %get-tuple-element.223), channel_id=1, source_target_pairs={{0,3},{1,4},{2,5},{3,6},{4,7},{5,8},{6,9},{7,10},{8,11},{9,12},{10... | collective-permute-start | bytes 196616 | tf_op jit(solution)/shard_map/while/body/eval_jaxpr/ppermute | solution.py:486
  65.6 8.5 %collective-permute-start.5 = (bf16[16,16,128]{2,1,0:T(8,128)(2,1)S(1)}, bf16[16,16,128]{2,1,0:T(8,128)(2,1)S(1)}, u32[]{:S(2)}, u32[]{:S(2)}) collective-permute-start(bf16[16,16,128]{2,1,0:T(8,128)(2,1)S(1)} %add_convert_fusion.2), channel_id=1, source_target_pairs={{0,4},{1,5},{2,6},{3,7},{4,8},{5,9},{6,10},{7,11},{8,12},{9,13},{1... | collective-permute-start | bytes 196616 | tf_op jit(solution)/shard_map/while/body/eval_jaxpr/ppermute | solution.py:486
  69.1 6.1 %collective-permute-start.4 = (bf16[16,16,128]{2,1,0:T(8,128)(2,1)S(1)}, bf16[16,16,128]{2,1,0:T(8,128)(2,1)S(1)}, u32[]{:S(2)}, u32[]{:S(2)}) collective-permute-start(bf16[16,16,128]{2,1,0:T(8,128)(2,1)S(1)} %add_convert_fusion.2), channel_id=1, source_target_pairs={{0,8},{1,9},{2,10},{3,11},{4,12},{5,13},{6,14},{7,15},{16,24},{17,... | collective-permute-start | bytes 196616 | tf_op jit(solution)/shard_map/while/body/eval_jaxpr/ppermute | solution.py:486
  72.8 3.8 %collective-permute-start.3 = (bf16[16,16,128]{2,1,0:T(8,128)(2,1)S(1)}, bf16[16,16,128]{2,1,0:T(8,128)(2,1)S(1)}, u32[]{:S(2)}, u32[]{:S(2)}) collective-permute-start(bf16[16,16,128]{2,1,0:T(8,128)(2,1)S(1)} %add_convert_fusion.2), channel_id=1, source_target_pairs={{0,12},{1,13},{2,14},{3,15},{16,28},{17,29},{18,30},{19,31}} | collective-permute-start | bytes 196616 | tf_op jit(solution)/shard_map/while/body/eval_jaxpr/ppermute | solution.py:486
  128.0 5.9 %collective-permute-start.2 = (bf16[16,16,128]{2,1,0:T(8,128)(2,1)}, bf16[16,16,128]{2,1,0:T(8,128)(2,1)S(1)}, u32[]{:S(2)}, u32[]{:S(2)}) collective-permute-start(bf16[16,16,128]{2,1,0:T(8,128)(2,1)} %get-tuple-element.223), channel_id=1, source_target_pairs={{0,1},{1,2},{2,3},{3,4},{4,5},{5,6},{6,7},{7,8},{8,9},{9,10},{10,1... | collective-permute-start | bytes 196616 | tf_op jit(solution)/shard_map/while/body/eval_jaxpr/ppermute | solution.py:486
  130.0 4.9 %collective-permute-start.1 = (bf16[16,16,128]{2,1,0:T(8,128)(2,1)}, bf16[16,16,128]{2,1,0:T(8,128)(2,1)S(1)}, u32[]{:S(2)}, u32[]{:S(2)}) collective-permute-start(bf16[16,16,128]{2,1,0:T(8,128)(2,1)} %get-tuple-element.223), channel_id=1, source_target_pairs={{0,2},{1,3},{2,4},{3,5},{4,6},{5,7},{6,8},{7,9},{8,10},{9,11},{10,... | collective-permute-start | bytes 196616 | tf_op jit(solution)/shard_map/while/body/eval_jaxpr/ppermute | solution.py:486
  132.6 3.5 %collective-permute-start = (bf16[16,16,128]{2,1,0:T(8,128)(2,1)}, bf16[16,16,128]{2,1,0:T(8,128)(2,1)S(1)}, u32[]{:S(2)}, u32[]{:S(2)}) collective-permute-start(bf16[16,16,128]{2,1,0:T(8,128)(2,1)} %get-tuple-element.223), channel_id=1, source_target_pairs={{0,3},{1,4},{2,5},{3,6},{4,7},{5,8},{6,9},{7,10},{8,11},{9,12},{10... | collective-permute-start | bytes 196616 | tf_op jit(solution)/shard_map/while/body/eval_jaxpr/ppermute | solution.py:486
  137.1 12.7 %collective-permute-start.5 = (bf16[16,16,128]{2,1,0:T(8,128)(2,1)S(1)}, bf16[16,16,128]{2,1,0:T(8,128)(2,1)S(1)}, u32[]{:S(2)}, u32[]{:S(2)}) collective-permute-start(bf16[16,16,128]{2,1,0:T(8,128)(2,1)S(1)} %add_convert_fusion.2), channel_id=1, source_target_pairs={{0,4},{1,5},{2,6},{3,7},{4,8},{5,9},{6,10},{7,11},{8,12},{9,13},{1... | collective-permute-start | bytes 196616 | tf_op jit(solution)/shard_map/while/body/eval_jaxpr/ppermute | solution.py:486
  143.4 7.4 %collective-permute-start.4 = (bf16[16,16,128]{2,1,0:T(8,128)(2,1)S(1)}, bf16[16,16,128]{2,1,0:T(8,128)(2,1)S(1)}, u32[]{:S(2)}, u32[]{:S(2)}) collective-permute-start(bf16[16,16,128]{2,1,0:T(8,128)(2,1)S(1)} %add_convert_fusion.2), channel_id=1, source_target_pairs={{0,8},{1,9},{2,10},{3,11},{4,12},{5,13},{6,14},{7,15},{16,24},{17,... | collective-permute-start | bytes 196616 | tf_op jit(solution)/shard_map/while/body/eval_jaxpr/ppermute | solution.py:486
  148.4 3.8 %collective-permute-start.3 = (bf16[16,16,128]{2,1,0:T(8,128)(2,1)S(1)}, bf16[16,16,128]{2,1,0:T(8,128)(2,1)S(1)}, u32[]{:S(2)}, u32[]{:S(2)}) collective-permute-start(bf16[16,16,128]{2,1,0:T(8,128)(2,1)S(1)} %add_convert_fusion.2), channel_id=1, source_target_pairs={{0,12},{1,13},{2,14},{3,15},{16,28},{17,29},{18,30},{19,31}} | collective-permute-start | bytes 196616 | tf_op jit(solution)/shard_map/while/body/eval_jaxpr/ppermute | solution.py:486

commit v3 on v1

--- a/solution.py
+++ b/solution.py
@@ -193,7 +193,7 @@
             pass
 
 
-BLOCK = 32
+BLOCK = 16
 
 
 def run_space(latent, embed, rows_of, input_weight, output_weight, out, places, ready):

time: 152 us -> 162 us (1.066)
  Pallas kernels: 101 us -> 110 us
    pallas_call x2, Pallas kernels: 97.7 us -> 107 us  [step_fused(): pl.pallas_call(fused_kernel, out_shape=[jax.ShapeDtypeStruct(latent.shape...]
where the time goes in v3:
time: 162 us; the launch traced here: 161 us
  Pallas kernels  110 us (68%)
  blocking collectives  25.5 us (16%)
  waiting for transfers between devices  13.7 us (8%)
  starting transfers between devices  6.98 us (4%)
  other arithmetic  3.21 us (2%)
    pallas_call x2, Pallas kernels, step_fused(): pl.pallas_call(fused_kernel, out_shape=[jax.ShapeDtypeStruct(latent.shape...  107 us
    all_to_all x2, blocking collectives, sum_before(): swap(held.reshape(rows, spatial))  25.5 us
    all_to_all x2, waiting for transfers between devices, sum_before(): return swap(sums.reshape(rows, spatial)).reshape(held.shape).astype(F32)  13.7 us
    all_to_all x2, starting transfers between devices, sum_before(): return swap(sums.reshape(rows, spatial)).reshape(held.shape).astype(F32)  6.98 us
  transfers between devices with their start and end apart: 2, of which 2 were waited for; matrix products, arithmetic and copies ran while one was open for 0% of the time, Pallas kernels for 0%

profile of v3, /device:TPU:0, one launch (start us, length us, event | category | flops | bytes accessed | tf_op | source)
XLA Modules:
  0.0 161.2 jit_solution(17618407251668942242)
XLA Ops:
  0.0 0.9 copy.24
  0.9 0.7 copy.15
  1.6 159.6 %while.12 = (s32[]{:T(128)}, f32[16,16,128]{2,1,0:T(8,128)S(1)}, f32[16,16,128]{2,1,0:T(8,128)}, pred[]{:T(512)}, s32[1]{0:T(128)}, /*index=5*/f32[16]{0:T(128)}...) while((s32[]{:T(128)}, f32[16,16,128]{2,1,0:T(8,128)S(1)}, ...), condition=%wide.region_1.2_spmd, body=%wide.region_0.1_spmd.sunk | while | flops 98306 | bytes 917694 | solution.py:529
  1.6 53.6 %denoise.1 = (f32[16,16,128]{2,1,0:T(8,128)}, bf16[16,16,128]{2,1,0:T(8,128)(2,1)}) custom-call(s32[1]{0:T(128)} %get-tuple-element.264.timestep, f32[16]{0:T(128)} %get-tuple-element.265.rate_state, f32[16]{0:T(128)} %get-tuple-element.266.rate_denoise, f32[16]{0:T(128)} %get-tuple-element.267.rate_noise, f32[16,16,128]{2,1,0:T(8,128)S(1)} %get-tuple-element.244.latent, ...), custom_call_target="tpu_custom_call" | custom-call | tf_op jit(solution)/shard_map/while/body/eval_jaxpr/denoise/pallas_call | solution.py:391
  55.2 14.4 %all_to_all.14.parts = bf16[16,16,128]{2,1,0:T(8,128)(2,1)} all-to-all(bf16[16,16,128]{2,1,0:T(8,128)(2,1)} %get-tuple-element.223), channel_id=1, replica_groups=mesh['group'=2,'tok'=16] {'tok'}, dimensions={0} | all-to-all | bytes 131072 | tf_op jit(solution)/shard_map/while/body/eval_jaxpr/all_to_all | solution.py:482
  69.6 1.5 earlier.1
  71.1 3.5 %all-to-all-start.1 = ((bf16[16,16,128]{2,1,0:T(8,128)(2,1)}), bf16[16,16,128]{2,1,0:T(8,128)(2,1)S(1)}, u32[]{:S(2)}, u32[]{:S(2)}) async-start(bf16[16,16,128]{2,1,0:T(8,128)(2,1)} %earlier.1), calls=%async_computation.1 | async-start | bytes 131072 | tf_op jit(solution)/shard_map/while/body/eval_jaxpr/all_to_all | solution.py:490
  74.6 6.9 %all-to-all-done.1 = bf16[16,16,128]{2,1,0:T(8,128)(2,1)S(1)} async-done(((bf16[16,16,128]{2,1,0:T(8,128)(2,1)}), bf16[16,16,128]{2,1,0:T(8,128)(2,1)S(1)}, u32[]{:S(2)}, u32[]{:S(2)}) %all-to-all-start.1) | async-done | bytes 65568 | tf_op jit(solution)/shard_map/while/body/eval_jaxpr/all_to_all | solution.py:490
  81.4 1.6 convert_add_fusion.2
  83.0 53.6 %denoise.1 = (f32[16,16,128]{2,1,0:T(8,128)}, bf16[16,16,128]{2,1,0:T(8,128)(2,1)}) custom-call(s32[1]{0:T(128)} %get-tuple-element.264.timestep, f32[16]{0:T(128)} %get-tuple-element.265.rate_state, f32[16]{0:T(128)} %get-tuple-element.266.rate_denoise, f32[16]{0:T(128)} %get-tuple-element.267.rate_noise, f32[16,16,128]{2,1,0:T(8,128)S(1)} %get-tuple-element.244.latent, ...), custom_call_target="tpu_custom_call" | custom-call | tf_op jit(solution)/shard_map/while/body/eval_jaxpr/denoise/pallas_call | solution.py:391
  136.7 11.1 %all_to_all.14.parts = bf16[16,16,128]{2,1,0:T(8,128)(2,1)} all-to-all(bf16[16,16,128]{2,1,0:T(8,128)(2,1)} %get-tuple-element.223), channel_id=1, replica_groups=mesh['group'=2,'tok'=16] {'tok'}, dimensions={0} | all-to-all | bytes 131072 | tf_op jit(solution)/shard_map/while/body/eval_jaxpr/all_to_all | solution.py:482
  147.7 1.5 earlier.1
  149.2 3.5 %all-to-all-start.1 = ((bf16[16,16,128]{2,1,0:T(8,128)(2,1)}), bf16[16,16,128]{2,1,0:T(8,128)(2,1)S(1)}, u32[]{:S(2)}, u32[]{:S(2)}) async-start(bf16[16,16,128]{2,1,0:T(8,128)(2,1)} %earlier.1), calls=%async_computation.1 | async-start | bytes 131072 | tf_op jit(solution)/shard_map/while/body/eval_jaxpr/all_to_all | solution.py:490
  152.7 6.9 %all-to-all-done.1 = bf16[16,16,128]{2,1,0:T(8,128)(2,1)S(1)} async-done(((bf16[16,16,128]{2,1,0:T(8,128)(2,1)}), bf16[16,16,128]{2,1,0:T(8,128)(2,1)S(1)}, u32[]{:S(2)}, u32[]{:S(2)}) %all-to-all-start.1) | async-done | bytes 65568 | tf_op jit(solution)/shard_map/while/body/eval_jaxpr/all_to_all | solution.py:490
  159.6 1.6 convert_add_fusion.2
Async XLA Ops:
  71.1 10.4 %all-to-all-start.1 = ((bf16[16,16,128]{2,1,0:T(8,128)(2,1)}), bf16[16,16,128]{2,1,0:T(8,128)(2,1)S(1)}, u32[]{:S(2)}, u32[]{:S(2)}) async-start(bf16[16,16,128]{2,1,0:T(8,128)(2,1)} %earlier.1), calls=%async_computation.1 | async-start | bytes 131072 | tf_op jit(solution)/shard_map/while/body/eval_jaxpr/all_to_all | solution.py:490
  149.2 10.4 %all-to-all-start.1 = ((bf16[16,16,128]{2,1,0:T(8,128)(2,1)}), bf16[16,16,128]{2,1,0:T(8,128)(2,1)S(1)}, u32[]{:S(2)}, u32[]{:S(2)}) async-start(bf16[16,16,128]{2,1,0:T(8,128)(2,1)} %earlier.1), calls=%async_computation.1 | async-start | bytes 131072 | tf_op jit(solution)/shard_map/while/body/eval_jaxpr/all_to_all | solution.py:490
